TPU v7x, 32 devices: a whole 2x2x4 slice. The times are simulated.
32 devices in a mesh: seq: 8 (over z, y), head: 4 (over x, core).
Axes of the slice: x: 2, y: 2, z: 4, core: 2. Of those that a mesh axis runs over, the one named last changes fastest.
Arguments:
- mamba_inner: bfloat16 [1024, 3072], P('seq', 'head'), may hold values from -6 to 6
- mamba_groups: bfloat16 [1024, 512], P('seq'), may hold values from -6 to 6
- selective_gate: bfloat16 [1024, 3072], P('seq', 'head'), may hold values from -6 to 6
- step_raw: float32 [48, 1024], P('head', 'seq'), may hold values from -3 to 3
- step_bias: float32 [48], P('head'), may hold values from -0.5 to 0.5
- decay_log: float32 [48], P('head'), may hold values from -12 to -2
- conv_inner: float32 [4, 3072], P(None, 'head'), may hold values from -3 to 3
- conv_groups: float32 [4, 512], replicated, may hold values from -3 to 3
- gated_norm_gain: float32 [3072], P('head'), may hold values from 0.1 to 1.9
- query_rows: bfloat16 [1024, 1024], P('seq', 'head'), may hold values from -8 to 8
- key_rows: bfloat16 [1024, 256], P('seq'), may hold values from -8 to 8
- value_rows: bfloat16 [1024, 256], P('seq'), may hold values from -6 to 6
- segment_ids: int32 [1024], P('seq'), may hold values from 0 to 15, never falling along the last dimension, each value on 1 to 682 neighbouring positions
- mamba_proj: bfloat16 [3072, 2048], P('head'), may hold values from -0.109375 to 0.109375
- attn_proj: bfloat16 [1024, 2048], P('head'), may hold values from -0.1875 to 0.1875
Outputs:
- mixed: bfloat16 [1024, 2048], P('seq', 'head')
Inputs may be any that keep to these rules, and one draw needn't show every extreme that they name: `segment_ids`: prompt numbers never fall along the tokens; each prompt holds 1 to 682 tokens and one holds exactly 682.
All inputs are finite; a program needn't handle non-finite values.
Results may differ from a plain program's by a relative error of at most 0.015.
Values may be sent and summed in bfloat16 or wider, within the bound.
A program may use at most 128 MiB of HBM per device.

v0:
```python
import math
import jax
import jax.numpy as jnp
from jax import lax
from jax.sharding import PartitionSpec as P

HEAD_CHANNELS = 64
STATE_SIZE = 256
QH = 8
KVH = 2
HD = 128


def shifted(value, axis, steps):
    count = lax.axis_size(axis)
    first, last = (max(0, -steps), min(count, count - steps))
    return lax.ppermute(value, axis, [(source, source + steps) for source in range(first, last)])


def entering(array, axis, combine, identity):
    length, position = (lax.axis_size(axis), lax.axis_index(axis))
    everything = jax.tree.map(
        lambda part, kind: lax.all_gather(part.astype(kind), axis),
        array,
        (jnp.bfloat16, jnp.bfloat16),
    )
    start = jax.tree.map(
        lambda part, zero: jnp.broadcast_to(jnp.asarray(zero, part.dtype), part.shape),
        array,
        identity,
    )

    def turn(k, before):
        reached = k < position
        new = combine(
            before, jax.tree.map(lambda part, own: part[k].astype(own.dtype), everything, array)
        )
        return jax.tree.map(lambda a, b: jnp.where(reached, a, b), new, before)

    return lax.fori_loop(0, length, turn, start)


def conv_silu(rows, weight, segs, rim_rows, rim_segs):
    item_count = rows.shape[0]
    padded = jnp.concatenate([rim_rows.astype(jnp.float32), rows.astype(jnp.float32)], 0)
    seg_pad = jnp.concatenate([rim_segs, segs], 0)
    total = jnp.zeros(rows.shape, jnp.float32)
    for offset in range(weight.shape[0]):
        window = padded[offset : offset + item_count]
        keep = (seg_pad[offset : offset + item_count] == segs).astype(jnp.float32)
        total = total + weight[offset][None, :] * window * keep[:, None]
    return jax.nn.silu(total).astype(jnp.bfloat16)


def mamba_local(inner, groups, segs, steps, rates, prev_last):
    highest = lax.Precision.HIGHEST
    cumul = jnp.cumsum(-steps * rates[:, None], axis=1)
    read_b = groups[:, :STATE_SIZE]
    read_c = groups[:, STATE_SIZE:]
    intersection = jnp.dot(read_c, read_b.T, preferred_element_type=jnp.float32)
    order = jnp.arange(segs.shape[0], dtype=jnp.int32)
    live = (segs[:, None] == segs[None, :]) & (order[:, None] >= order[None, :])
    decays = jnp.exp(jnp.where(live[None], cumul[:, :, None] - cumul[:, None, :], -jnp.inf))
    mixing = intersection[None] * decays
    scaled = inner.astype(jnp.float32) * steps.T[:, :, None]
    output = jnp.einsum("htj,jhd->thd", mixing, scaled, precision=highest)
    tail = jnp.exp(cumul[:, -1:] - cumul) * (segs == segs[-1]).astype(jnp.float32)[None, :]
    local_state = jnp.einsum(
        "ht,thd,tn->hdn", tail, scaled, read_b.astype(jnp.float32), precision=highest
    )
    through = jnp.exp(cumul[:, -1]) * (segs[-1] == prev_last).astype(jnp.float32)
    return (output, through, local_state, cumul)


def mamba_incoming(output, incoming, groups, segs, cumul, prev_last):
    read_c = groups[:, STATE_SIZE:].astype(jnp.float32)
    joined = (segs == prev_last).astype(jnp.float32)
    from_carry = jnp.einsum("hdn,tn->thd", incoming, read_c, precision=lax.Precision.HIGHEST)
    return output + jnp.exp(cumul).T[:, :, None] * joined[:, None, None] * from_carry


def combine_states(earlier, later):
    return (earlier[0] * later[0], later[0][:, None, None] * earlier[1] + later[1])


def shards(
    mamba_inner,
    mamba_groups,
    selective_gate,
    step_raw,
    step_bias,
    decay_log,
    conv_inner,
    conv_groups,
    gated_norm_gain,
    query_rows,
    key_rows,
    value_rows,
    segment_ids,
    mamba_proj,
    attn_proj,
):
    item_count = segment_ids.shape[0]
    taps = conv_inner.shape[0]
    resident_heads = step_raw.shape[0]
    rim_inner, rim_groups, rim_marks = shifted(
        (
            mamba_inner[item_count - taps + 1 :],
            mamba_groups[item_count - taps + 1 :],
            segment_ids[item_count - taps + 1 :].astype(jnp.bfloat16),
        ),
        "seq",
        1,
    )
    rim_segs = rim_marks.astype(jnp.float32).astype(jnp.int32)
    prev_last = rim_segs[-1]
    inner_filtered = conv_silu(mamba_inner, conv_inner, segment_ids, rim_inner, rim_segs).reshape(
        item_count, resident_heads, HEAD_CHANNELS
    )
    groups_conv = conv_silu(mamba_groups, conv_groups, segment_ids, rim_groups, rim_segs)
    steps = jax.nn.softplus(step_raw + step_bias[:, None])
    rates = jnp.exp(decay_log)
    output, through, local_state, cumul = mamba_local(
        inner_filtered, groups_conv, segment_ids, steps, rates, prev_last
    )
    identity = (jnp.ones_like(through), jnp.zeros_like(local_state))
    carry_decay, carry_state = entering((through, local_state), "seq", combine_states, identity)
    selective_output = mamba_incoming(
        output, carry_state, groups_conv, segment_ids, cumul, prev_last
    )
    gated_values = selective_output * jax.nn.silu(selective_gate.astype(jnp.float32)).reshape(
        item_count, resident_heads, HEAD_CHANNELS
    )
    mean_square = jnp.mean(gated_values * gated_values, axis=-1, keepdims=True)
    normalized_rows = (
        (
            gated_values
            * lax.rsqrt(mean_square + 1e-05)
            * gated_norm_gain.reshape(resident_heads, HEAD_CHANNELS)
        )
        .astype(jnp.bfloat16)
        .reshape(item_count, resident_heads * HEAD_CHANNELS)
    )
    heads_here = query_rows.shape[1] // HD
    group_size = QH // KVH
    kv_index = lax.axis_index("head") * heads_here // group_size
    my_keys = lax.dynamic_slice_in_dim(key_rows, kv_index * HD, HD, 1)
    my_values = lax.dynamic_slice_in_dim(value_rows, kv_index * HD, HD, 1)
    marks = segment_ids.astype(jnp.bfloat16)
    block_start = lax.axis_index("seq") * item_count
    query_pos = block_start + jnp.arange(item_count, dtype=jnp.int32)
    queries = query_rows.reshape(item_count, heads_here, HD).transpose(1, 0, 2)
    scale = 1.0 / math.sqrt(HD)
    start_state = (
        jnp.full((heads_here, item_count), -1e30, jnp.float32),
        jnp.zeros((heads_here, item_count), jnp.float32),
        jnp.zeros((heads_here, item_count, HD), jnp.float32),
    )
    piece_keys = lax.all_gather(my_keys, "seq", axis=0, tiled=True)
    piece_values = lax.all_gather(my_values, "seq", axis=0, tiled=True)
    piece_marks = lax.all_gather(marks, "seq", axis=0, tiled=True)
    rows = piece_keys.shape[0]
    width = math.gcd(rows, item_count)
    blocks = rows // width

    def one_block(state, item):
        top, total, summed = state
        block_keys, block_values, block_marks, offset = item
        key_pos = offset * width + jnp.arange(width, dtype=jnp.int32)
        key_seg = block_marks.astype(jnp.float32).astype(jnp.int32)
        allowed = (
            (key_seg[None, :] == segment_ids[:, None])
            & (key_pos[None, :] <= query_pos[:, None])
            & (key_pos[None, :] >= 0)
        )
        scores = (
            jnp.einsum("hqd,kd->hqk", queries, block_keys, preferred_element_type=jnp.float32)
            * scale
        )
        scores = jnp.where(allowed[None], scores, -jnp.inf)
        new_top = jnp.maximum(top, jnp.max(scores, axis=-1))
        rescale = jnp.exp(top - new_top)
        weights = jnp.exp(scores - new_top[..., None])
        total = total * rescale + jnp.sum(weights, axis=-1)
        summed = summed * rescale[..., None] + jnp.einsum(
            "hqk,kd->hqd",
            weights.astype(jnp.bfloat16),
            block_values,
            preferred_element_type=jnp.float32,
        )
        return ((new_top, total, summed), None)

    items = (
        piece_keys.reshape(blocks, width, HD),
        piece_values.reshape(blocks, width, HD),
        piece_marks.reshape(blocks, width),
        jnp.arange(blocks, dtype=jnp.int32),
    )
    result, unused = lax.scan(one_block, start_state, items)
    top_final, total_final, summed_final = result
    attended = (
        (summed_final / total_final[..., None])
        .astype(jnp.bfloat16)
        .transpose(1, 0, 2)
        .reshape(item_count, heads_here * HD)
    )
    terms = jnp.dot(normalized_rows, mamba_proj, preferred_element_type=jnp.float32) + jnp.dot(
        attended, attn_proj, preferred_element_type=jnp.float32
    )
    return lax.psum_scatter(terms.astype(jnp.bfloat16), "head", scatter_dimension=1, tiled=True)


def solution(mesh):
    placed = (
        P("seq", "head"),
        P("seq", None),
        P("seq", "head"),
        P("head", "seq"),
        P("head"),
        P("head"),
        P(None, "head"),
        P(),
        P("head"),
        P("seq", "head"),
        P("seq", None),
        P("seq", None),
        P("seq"),
        P("head", None),
        P("head", None),
    )
    return jax.shard_map(
        shards, mesh=mesh, in_specs=placed, out_specs=P("seq", "head"), check_vma=False
    )
```

profile of v0, /device:TPU:0, one launch (start us, length us, event | category | flops | bytes accessed | tf_op | source)
XLA Modules:
  0.0 241.9 jit_solution(1705443980735956197)
XLA Ops:
  7.9 5.4 %collective-permute-start.1 = (bf16[3]{0:T(256)(128)(2,1)}, bf16[3]{0:T(256)(128)(2,1)}, u32[]{:S(2)}, u32[]{:S(2)}) collective-permute-start(bf16[3]{0:T(256)(128)(2,1)} %slice.85), channel_id=1, source_target_pairs={{0,4},{4,8},{8,12},{12,16},{16,20},{20,24},{24,28},{1,5},{5,9},{9,... | collective-permute-start | bytes 26 | tf_op jit(solution)/shard_map/ppermute | solution.py:17
  14.0 3.5 %collective-permute-start.2 = (bf16[3,512]{1,0:T(4,128)(2,1)S(1)}, bf16[3,512]{1,0:T(4,128)(2,1)}, u32[]{:S(2)}, u32[]{:S(2)}) collective-permute-start(bf16[3,512]{1,0:T(4,128)(2,1)S(1)} %slice.95), channel_id=1, source_target_pairs={{0,4},{4,8},{8,12},{12,16},{16,20},{20,24},{24,28},{1,5},{5,9},{9,... | collective-permute-start | bytes 9224 | tf_op jit(solution)/shard_map/ppermute | solution.py:17
  19.1 3.5 %collective-permute-start = (bf16[3,768]{0,1:T(8,128)(2,1)}, bf16[3,768]{0,1:T(8,128)(2,1)}, u32[]{:S(2)}, u32[]{:S(2)}) collective-permute-start(bf16[3,768]{0,1:T(8,128)(2,1)} %copy.27), channel_id=1, source_target_pairs={{0,4},{4,8},{8,12},{12,16},{16,20},{20,24},{24,28},{1,5},{5,9},{9,... | collective-permute-start | bytes 13832 | tf_op jit(solution)/shard_map/ppermute | solution.py:17
  22.6 1.2 slice.106
  23.8 1.6 convert_element_type.131
  25.5 1.1 copy.28
  31.8 32.9 %all_gather.23 = bf16[1024,128]{1,0:T(8,128)(2,1)} all-gather(bf16[128,128]{1,0:T(8,128)(2,1)S(1)} %constant_dynamic-slice_fusion.2), channel_id=1, replica_groups=mesh['seq'=8,'head'=4] {'seq'}, dimensions={0}, use_global_device_ids=true | all-gather | bytes 294912 | tf_op jit(solution)/shard_map/all_gather | solution.py:159
  65.5 32.9 %all_gather.24 = bf16[1024,128]{1,0:T(8,128)(2,1)} all-gather(bf16[128,128]{1,0:T(8,128)(2,1)S(1)} %constant_dynamic-slice_fusion.1), channel_id=1, replica_groups=mesh['seq'=8,'head'=4] {'seq'}, dimensions={0}, use_global_device_ids=true | all-gather | bytes 294912 | tf_op jit(solution)/shard_map/all_gather | solution.py:160
  98.4 16.8 %all-gather.2 = bf16[8,1,128]{2,1,0:T(2,128)(2,1)S(1)} all-gather(bf16[1,1,128]{2,1,0:T(2,128)(2,1)S(1)} %get-tuple-element.295), channel_id=1, replica_groups=mesh['seq'=8,'head'=4] {'seq'}, dimensions={0}, use_global_device_ids=true | all-gather | bytes 2304 | tf_op jit(solution)/shard_map/all_gather | solution.py:161
  115.8 0.9 copy.30
  118.8 2.0 compare_convert_fusion.4
  122.1 1.6 multiply_convert_fusion.2
  123.7 1.0 convert_element_type.120
  124.7 2.5 %multiply_convert_fusion.1 = bf16[128,768]{0,1:T(8,128)(2,1)S(1)} fusion(f32[128,768]{0,1:T(8,128)} %convert_element_type.121, f32[3,768]{0,1:T(8,128)S(1)} %convert_element_type.120, f32[768]{0:T(1024)S(1)} %get-tuple-element.241, f32[128]{0:T(128)S(1)} %get-tuple-element.290, f32[768]{0:T(1024)S(1)} %get-tuple-element.242, f32[128]{0:T(128)S(1)} %get-tuple-element.291, ...), kind=kLoop, calls=%fused_computation.74 | loop fusion | flops 1769472 | bytes 612864 | tf_op jit(solution)/shard_map/convert_element_type | solution.py:52
  127.9 1.2 convolution_convert_fusion
  129.2 32.5 %while.30 = (s32[]{:T(128)}, f32[2,128]{1,0:T(2,128)S(1)}, f32[2,128]{1,0:T(2,128)S(1)}, f32[2,128,128]{2,1,0:T(8,128)S(1)}, bf16[8,128]{1,0:T(8,128)(2,1)}, /*i...) while((s32[]{:T(128)}, f32[2,128]{1,0:T(2,128)S(1)}, ...), condition=%wide.region_7.8_spmd.clone, body=%wide.region_4.7_spmd.clone.sunk | while | flops 17172484 | bytes 840889 | solution.py:199
  132.2 1.0 convolution_add_fusion.3
  135.3 0.9 fusion.97
  136.3 1.0 convolution_add_fusion.3
  139.3 0.9 fusion.97
  140.4 1.0 convolution_add_fusion.3
  143.4 0.9 fusion.97
  144.4 1.0 convolution_add_fusion.3
  148.5 1.0 convolution_add_fusion.3
  151.5 0.9 fusion.97
  152.5 1.0 convolution_add_fusion.3
  155.6 0.9 fusion.97
  156.6 1.0 convolution_add_fusion.3
  159.6 1.0 fusion.97
  160.7 1.0 convolution_add_fusion.3
  161.7 1.8 copy.29
  164.3 1.3 dynamic-slice
  166.4 1.8 convert_multiply_fusion
  168.2 2.6 %fusion.76 = f32[128,2048]{1,0:T(8,128)} fusion(bf16[128,256]{0,1:T(8,128)(2,1)S(1)} %bitcast.93, bf16[256,2048]{1,0:T(8,128)(2,1)} %param.33), kind=kOutput, calls=%fused_computation.132 | convolution fusion | flops 134217728 | bytes 2162688 | tf_op jit(solution)/shard_map/dot_general | solution.py:207
  172.5 18.7 %all-reduce = bf16[96]{0:T(256)(128)(2,1)S(1)} all-reduce(bf16[96]{0:T(256)(128)(2,1)S(1)} %dynamic-update-slice), channel_id=2, replica_groups=mesh['seq'=8,'head'=4] {'seq'}, use_global_device_ids=true, to_apply=%add | all-reduce | flops 96 | bytes 384
  191.4 18.2 %while.29 = (s32[]{:T(128)}, f32[12,64,256]{2,1,0:T(8,128)}, s32[]{:T(128)}, bf16[8,12]{1,0:T(8,128)(2,1)S(1)}, bf16[8,12,64,256]{3,2,1,0:T(8,128)(2,1)}, /*index=5*/s32[]{:T(128)}, s32[]{:T(128)}) while((s32[]{:T(128)}, f32[12,64,256]{2,1,0:T(8,128)}, s32[]{:T(128)}, bf16[8,12]{1,0:T(8,128)(2,1)S(1)}, ...), condition=%wide.region_2.3_spmd.clone, body=%wide.region_1.2_spmd.clone.sunk | while | flops 983056 | bytes 1966305 | solution.py:40
  191.5 2.1 fusion.92
  193.5 2.3 fusion.92
  195.8 2.3 fusion.92
  198.1 2.3 fusion.92
  200.4 2.3 fusion.92
  202.7 2.3 fusion.92
  205.0 2.3 fusion.92
  207.3 2.3 fusion.92
  209.6 1.7 convolution_multiply_fusion.1
  211.3 2.8 %multiply_reduce_fusion = (f32[128,12]{0,1:T(8,128)S(1)}, f32[128,12,64]{0,2,1:T(8,128)S(1)}) fusion(f32[128,12,64]{0,2,1:T(8,128)} %bitcast.92, f32[128,12,64]{0,2,1:T(8,128)S(1)} %convolution_multiply_fusion.1, f32[12,128]{1,0:T(8,128)S(1)} %reduce_window_sum.11, f32[128,128]{1,0:T(8,128)S(1)} %fusion.66, pred[128,128]{1,0:T(8,128)(4,1)S(1)} %fusion.64, ...), kind=kOutput, calls=%fused_computation.69 | convolution fusion | flops 152173056 | bytes 1476608 | tf_op jit(solution)/shard_map/htj,jhd->thd/dot_general | solution.py:66
  214.4 1.4 fusion.20
  215.8 19.3 %reduce-scatter.2.cloned.1.call-done = bf16[128,512]{1,0:T(8,128)(2,1)} async-done(((bf16[128,2048]{1,0:T(8,128)(2,1)}), bf16[128,512]{1,0:T(8,128)(2,1)}) %reduce-scatter.2.cloned.1.call-update) | async-done | bytes 131088 | tf_op jit(solution)/shard_map/reduce_scatter | solution.py:210
  (149 shorter events, 29.9 us)
Async XLA Ops:
  6.5 207.8 %copy-start = (bf16[768,2048]{1,0:T(8,128)(2,1)S(1)}, bf16[768,2048]{1,0:T(8,128)(2,1)}, u32[]{:S(2)}) copy-start(bf16[768,2048]{1,0:T(8,128)(2,1)} %param.32) | copy-start | bytes 9437188
  6.5 122.6 %copy-start.5 = (s32[128]{0:T(128)S(1)}, s32[128]{0:T(128)}, u32[]{:S(2)}) copy-start(s32[128]{0:T(128)} %param.31) | copy-start | bytes 1540
  6.5 184.9 %all-gather.5.cloned.1.call-start = ((), (), s32[]{:S(2)}) async-start(), calls=%async_computation.2 | async-start | bytes 3538944 | tf_op jit(solution)/shard_map/all_gather | solution.py:23
  7.9 108.9 %collective-permute-start.1 = (bf16[3]{0:T(256)(128)(2,1)}, bf16[3]{0:T(256)(128)(2,1)}, u32[]{:S(2)}, u32[]{:S(2)}) collective-permute-start(bf16[3]{0:T(256)(128)(2,1)} %slice.85), channel_id=1, source_target_pairs={{0,4},{4,8},{8,12},{12,16},{16,20},{20,24},{24,28},{1,5},{5,9},{9,... | collective-permute-start | bytes 26 | tf_op jit(solution)/shard_map/ppermute | solution.py:17
  14.0 107.4 %collective-permute-start.2 = (bf16[3,512]{1,0:T(4,128)(2,1)S(1)}, bf16[3,512]{1,0:T(4,128)(2,1)}, u32[]{:S(2)}, u32[]{:S(2)}) collective-permute-start(bf16[3,512]{1,0:T(4,128)(2,1)S(1)} %slice.95), channel_id=1, source_target_pairs={{0,4},{4,8},{8,12},{12,16},{16,20},{20,24},{24,28},{1,5},{5,9},{9,... | collective-permute-start | bytes 9224 | tf_op jit(solution)/shard_map/ppermute | solution.py:17
  19.1 104.6 %collective-permute-start = (bf16[3,768]{0,1:T(8,128)(2,1)}, bf16[3,768]{0,1:T(8,128)(2,1)}, u32[]{:S(2)}, u32[]{:S(2)}) collective-permute-start(bf16[3,768]{0,1:T(8,128)(2,1)} %copy.27), channel_id=1, source_target_pairs={{0,4},{4,8},{8,12},{12,16},{16,20},{20,24},{24,28},{1,5},{5,9},{9,... | collective-permute-start | bytes 13832 | tf_op jit(solution)/shard_map/ppermute | solution.py:17
  30.6 98.6 %copy-start.6 = (f32[128,12]{0,1:T(8,128)}, f32[128,12]{0,1:T(8,128)S(1)}, u32[]{:S(2)}) copy-start(f32[128,12]{0,1:T(8,128)S(1)} %get-tuple-element.281) | copy-start | bytes 18436
  123.7 3.5 %copy-start.2 = (bf16[128,512]{1,0:T(8,128)(2,1)}, bf16[128,512]{1,0:T(8,128)(2,1)S(1)}, u32[]{:S(2)}) copy-start(bf16[128,512]{1,0:T(8,128)(2,1)S(1)} %multiply_convert_fusion.2) | copy-start | bytes 393220
  127.2 0.7 copy-start.4
  127.2 36.3 %copy-start.10 = (f32[768]{0:T(1024)S(1)}, f32[768]{0:T(1024)}, u32[]{:S(2)}) copy-start(f32[768]{0:T(1024)} %param.27) | copy-start | bytes 9220
  129.1 106.0 %reduce-scatter.2.cloned.1.call-start = ((), (), s32[]{:S(2)}) async-start(), calls=%async_computation.1 | async-start | bytes 655360 | tf_op jit(solution)/shard_map/reduce_scatter | solution.py:210
  161.7 29.6 %copy-start.3 = (bf16[128,512]{1,0:T(8,128)(2,1)S(1)}, bf16[128,512]{1,0:T(8,128)(2,1)}, u32[]{:S(2)}) copy-start(bf16[128,512]{1,0:T(8,128)(2,1)} %copy-done.2) | copy-start | bytes 393220
  191.4 18.2 %copy-start.8 = (f32[128,12]{0,1:T(8,128)S(1)}, f32[128,12]{0,1:T(8,128)}, u32[]{:S(2)}) copy-start(f32[128,12]{0,1:T(8,128)} %get-tuple-element.283) | copy-start | bytes 18436
  191.4 19.9 %copy-start.7 = (f32[128,12]{0,1:T(8,128)S(1)}, f32[128,12]{0,1:T(8,128)}, u32[]{:S(2)}) copy-start(f32[128,12]{0,1:T(8,128)} %copy-done.6) | copy-start | bytes 18436
  191.4 22.7 %copy-start.9 = (f32[12,64]{1,0:T(8,128)S(1)}, f32[12,64]{1,0:T(8,128)}, u32[]{:S(2)}) copy-start(f32[12,64]{1,0:T(8,128)} %mul.345) | copy-start | bytes 9220
  209.6 4.7 %copy-start.1 = (f32[128,2048]{1,0:T(8,128)S(1)}, f32[128,2048]{1,0:T(8,128)}, u32[]{:S(2)}) copy-start(f32[128,2048]{1,0:T(8,128)} %fusion.76) | copy-start | bytes 3145732
Sparse Core Ops, SparseCore 0:
  129.2 58.6 all-gather.4
  215.9 19.1 reduce-scatter.1
where the time goes:
time: 244 us; the launch traced here: 242 us
  blocking collectives  101 us (41%)
  other arithmetic  41.5 us (17%)
  matrix products  25.3 us (10%)
  local copies, waits for them, and re-layouts  21.2 us (9%)
  waiting for transfers between devices  19.4 us (8%)
  between operations  15.7 us (6%)
  starting transfers between devices  12.4 us (5%)
  loops' own time  5.2 us (2%)
    all_gather x1, blocking collectives, shards(): piece_keys = lax.all_gather(my_keys, 'seq', axis=0, tiled=True)  32.9 us
    all_gather x1, blocking collectives, shards(): piece_values = lax.all_gather(my_values, 'seq', axis=0, tiled=True)  32.9 us
    reduce_scatter x1, waiting for transfers between devices, shards(): lax.psum_scatter(terms.astype(jnp.bfloat16), 'head', scatter_dimension=1,...  19.3 us
    unnamed x1, blocking collectives  18.7 us
    select_n x8, other arithmetic, turn(): return jax.tree.map(lambda a, b: jnp.where(reached, a, b), new, before)  18.1 us
    all_gather x1, blocking collectives, shards(): piece_marks = lax.all_gather(marks, 'seq', axis=0, tiled=True)  16.8 us
    ppermute x3, starting transfers between devices, shifted(): lax.ppermute(value, axis, [(source, source + steps) for source in range(f...  12.4 us
    dot_general x8, matrix products, one_block(): jnp.einsum('hqk,kd->hqd', weights.astype(jnp.bfloat16), block_values, pre...  7.87 us
  transfers between devices with their start and end apart: 5, of which 1 were waited for; matrix products, arithmetic and copies ran while one was open for 24% of the time, Pallas kernels for 0%

commit v1 on v0

--- a/solution.py
+++ b/solution.py
@@ -157,7 +157,26 @@
         jnp.zeros((heads_here, item_count, HD), jnp.float32),
     )
     piece_keys = lax.all_gather(my_keys, "seq", axis=0, tiled=True)
-    piece_values = lax.all_gather(my_values, "seq", axis=0, tiled=True)
+    size, index, extent = (lax.axis_size("seq"), lax.axis_index("seq"), my_values.shape[0])
+    ahead = [(i, (i + 1) % size) for i in range(size)]
+    left = [(i, (i - 1) % size) for i in range(size)]
+    whole = jnp.zeros(
+        (*my_values.shape[:0], size * extent, *my_values.shape[0 + 1 :]), my_values.dtype
+    )
+    whole = lax.dynamic_update_slice_in_dim(whole, my_values, index * extent, axis=0)
+    from_left = from_right = my_values
+    half = size // 2
+    for step in range(1, half + 1):
+        from_left = lax.ppermute(from_left, "seq", ahead)
+        whole = lax.dynamic_update_slice_in_dim(
+            whole, from_left, (index - step) % size * extent, axis=0
+        )
+        if step < size - half:
+            from_right = lax.ppermute(from_right, "seq", left)
+            whole = lax.dynamic_update_slice_in_dim(
+                whole, from_right, (index + step) % size * extent, axis=0
+            )
+    piece_values = whole
     piece_marks = lax.all_gather(marks, "seq", axis=0, tiled=True)
     rows = piece_keys.shape[0]
     width = math.gcd(rows, item_count)

time: 244 us -> 274 us (1.12)
  blocking collectives: 101 us -> 68.2 us
  other arithmetic: 41.5 us -> 69 us
  local copies, waits for them, and re-layouts: 21.2 us -> 36.3 us
  starting transfers between devices: 12.4 us -> 24 us
  waiting for transfers between devices: 19.4 us -> 26.4 us
    all_gather x1 -> x0, blocking collectives: 32.9 us -> none  [shards(): piece_values = lax.all_gather(my_values, 'seq', axis=0, tiled=True)]
    ppermute x0 -> x7, starting transfers between devices: none -> 15.5 us  [the longest x3 10.7 us: shards(): from_right = lax.ppermute(from_right, 'seq', left)]
    add x8, other arithmetic: 0.14 us -> 9.68 us  [one_block(): total = total * rescale + jnp.sum(weights, axis=-1)]
    convert_element_type x8, other arithmetic: 0.04 us -> 9.35 us  [turn(): part[k].astype(own.dtype)]
    dynamic_update_slice x0 -> x8, local copies, waits for them, and re-layouts: none -> 7.32 us  [the longest x4 3.19 us: shards(): lax.dynamic_update_slice_in_dim(whole, from_left, (index - step) % size *...]
    ppermute x0 -> x7, waiting for transfers between devices: none -> 7.28 us  [the longest x4 7.27 us: shards(): from_left = lax.ppermute(from_left, 'seq', ahead)]
    and x8, other arithmetic: 0.96 us -> 6.16 us  [one_block(): (key_seg[None, :] == segment_ids[:, None]) & (key_pos[None, :] <= query_p...]
    dynamic_slice x8, local copies, waits for them, and re-layouts: 4.73 us -> 9.82 us  [shards(): result, unused = lax.scan(one_block, start_state, items)]
  transfers between devices with their start and end apart: 5 -> 12, of which waited for: 1 -> 3; matrix products, arithmetic and copies ran while one was open for 24% -> 35% of each run, Pallas kernels for 0% -> 0%
where the time goes in v1:
time: 274 us; the launch traced here: 271 us
  other arithmetic  69 us (25%)
  blocking collectives  68.2 us (25%)
  local copies, waits for them, and re-layouts  36.3 us (13%)
  waiting for transfers between devices  26.4 us (10%)
  matrix products  25.8 us (9%)
  starting transfers between devices  24 us (9%)
  between operations  15.7 us (6%)
  loops' own time  5.47 us (2%)
    all_gather x1, blocking collectives, shards(): piece_keys = lax.all_gather(my_keys, 'seq', axis=0, tiled=True)  32.8 us
    reduce_scatter x1, waiting for transfers between devices, shards(): lax.psum_scatter(terms.astype(jnp.bfloat16), 'head', scatter_dimension=1,...  19 us
    select_n x8, other arithmetic, turn(): return jax.tree.map(lambda a, b: jnp.where(reached, a, b), new, before)  18.3 us
    all_gather x1, blocking collectives, shards(): piece_marks = lax.all_gather(marks, 'seq', axis=0, tiled=True)  18 us
    unnamed x1, blocking collectives  17.4 us
    ppermute x3, starting transfers between devices, shards(): from_right = lax.ppermute(from_right, 'seq', left)  10.7 us
    dynamic_slice x8, local copies, waits for them, and re-layouts, shards(): result, unused = lax.scan(one_block, start_state, items)  9.82 us
    add x8, other arithmetic, one_block(): total = total * rescale + jnp.sum(weights, axis=-1)  9.68 us
  transfers between devices with their start and end apart: 12, of which 3 were waited for; matrix products, arithmetic and copies ran while one was open for 35% of the time, Pallas kernels for 0%

profile of v1, /device:TPU:0, one launch (start us, length us, event | category | flops | bytes accessed | tf_op | source)
XLA Modules:
  0.0 270.8 jit_solution(12767234549833551922)
XLA Ops:
  7.3 1.6 constant_dynamic-update-slice_fusion.7
  8.8 3.0 %collective-permute-start.3 = (bf16[128,128]{1,0:T(8,128)(2,1)}, bf16[128,128]{1,0:T(8,128)(2,1)}, u32[]{:S(2)}, u32[]{:S(2)}) collective-permute-start(bf16[128,128]{1,0:T(8,128)(2,1)} %get-tuple-element.278), channel_id=1, source_target_pairs={{0,4},{4,8},{8,12},{12,16},{16,20},{20,24},{24,28},{28,0},{1,5},{5... | collective-permute-start | bytes 98312 | tf_op jit(solution)/shard_map/ppermute | solution.py:170
  11.8 3.0 %collective-permute-start.4 = (bf16[128,128]{1,0:T(8,128)(2,1)}, bf16[128,128]{1,0:T(8,128)(2,1)}, u32[]{:S(2)}, u32[]{:S(2)}) collective-permute-start(bf16[128,128]{1,0:T(8,128)(2,1)} %get-tuple-element.278), channel_id=1, source_target_pairs={{0,28},{4,0},{8,4},{12,8},{16,12},{20,16},{24,20},{28,24},{1,29},{... | collective-permute-start | bytes 98312 | tf_op jit(solution)/shard_map/ppermute | solution.py:175
  16.7 1.8 collective-permute-start.1
  19.8 4.0 %collective-permute-start.2 = (bf16[3,512]{1,0:T(4,128)(2,1)}, bf16[3,512]{1,0:T(4,128)(2,1)}, u32[]{:S(2)}, u32[]{:S(2)}) collective-permute-start(bf16[3,512]{1,0:T(4,128)(2,1)} %slice.95), channel_id=1, source_target_pairs={{0,4},{4,8},{8,12},{12,16},{16,20},{20,24},{24,28},{1,5},{5,9},{9,... | collective-permute-start | bytes 9224 | tf_op jit(solution)/shard_map/ppermute | solution.py:17
  25.4 2.6 collective-permute-start
  29.2 1.6 convert_element_type.131
  32.0 1.4 fusion.64
  33.4 1.5 fusion.74
  34.8 1.5 slice_reduce_fusion.4
  37.8 1.4 fusion.71
  42.1 1.3 mul.367
  44.2 32.8 %all_gather.20 = bf16[1024,128]{1,0:T(8,128)(2,1)} all-gather(bf16[128,128]{1,0:T(8,128)(2,1)S(1)} %constant_dynamic-slice_fusion.2), channel_id=1, replica_groups=mesh['seq'=8,'head'=4] {'seq'}, dimensions={0}, use_global_device_ids=true | all-gather | bytes 294912 | tf_op jit(solution)/shard_map/all_gather | solution.py:159
  77.0 18.0 %all-gather.2 = bf16[8,1,128]{2,1,0:T(2,128)(2,1)S(1)} all-gather(bf16[1,1,128]{2,1,0:T(2,128)(2,1)} %get-tuple-element.297), channel_id=1, replica_groups=mesh['seq'=8,'head'=4] {'seq'}, dimensions={0}, use_global_device_ids=true | all-gather | bytes 2304 | tf_op jit(solution)/shard_map/all_gather | solution.py:180
  95.9 1.3 dynamic-slice
  101.3 2.0 compare_convert_fusion.4
  105.0 17.4 %all-reduce = bf16[96]{0:T(256)(128)(2,1)S(1)} all-reduce(bf16[96]{0:T(256)(128)(2,1)S(1)} %dynamic-update-slice), channel_id=2, replica_groups=mesh['seq'=8,'head'=4] {'seq'}, use_global_device_ids=true, to_apply=%add | all-reduce | flops 96 | bytes 384
  123.7 1.5 multiply_convert_fusion.2
  126.3 2.5 multiply_convert_fusion.1
  129.5 1.9 convolution_convert_fusion
  131.5 1.9 collective-permute-start.5
  133.4 2.9 %collective-permute-start.6 = (bf16[128,128]{1,0:T(8,128)(2,1)}, bf16[128,128]{1,0:T(8,128)(2,1)S(1)}, u32[]{:S(2)}, u32[]{:S(2)}) collective-permute-start(bf16[128,128]{1,0:T(8,128)(2,1)} %collective-permute-done.4), channel_id=1, source_target_pairs={{0,28},{4,0},{8,4},{12,8},{16,12},{20,16},{24,20},{28,24},{1,29},{... | collective-permute-start | bytes 98312 | tf_op jit(solution)/shard_map/ppermute | solution.py:175
  136.3 1.4 constant_dynamic-update-slice_fusion.6
  137.7 1.4 constant_dynamic-update-slice_fusion.5
  139.1 4.7 %collective-permute-start.8 = (bf16[128,128]{1,0:T(8,128)(2,1)S(1)}, bf16[128,128]{1,0:T(8,128)(2,1)S(1)}, u32[]{:S(2)}, u32[]{:S(2)}) collective-permute-start(bf16[128,128]{1,0:T(8,128)(2,1)S(1)} %collective-permute-done.6), channel_id=1, source_target_pairs={{0,28},{4,0},{8,4},{12,8},{16,12},{20,16},{24,20},{28,24},{1,29},{... | collective-permute-start | bytes 98312 | tf_op jit(solution)/shard_map/ppermute | solution.py:175
  147.4 6.1 %collective-permute-done.9 = bf16[128,128]{1,0:T(8,128)(2,1)S(1)} collective-permute-done((bf16[128,128]{1,0:T(8,128)(2,1)S(1)}, bf16[128,128]{1,0:T(8,128)(2,1)S(1)}, u32[]{:S(2)}, u32[]{:S(2)}) %collective-permute-start.9) | collective-permute-done | bytes 32800 | tf_op jit(solution)/shard_map/ppermute | solution.py:170
  154.6 52.5 %while.30 = (s32[]{:T(128)}, f32[2,128]{1,0:T(2,128)S(1)}, f32[2,128]{1,0:T(2,128)}, f32[2,128,128]{2,1,0:T(8,128)S(1)}, bf16[8,128]{1,0:T(8,128)(2,1)}, /*index...) while((s32[]{:T(128)}, f32[2,128]{1,0:T(2,128)S(1)}, ...), condition=%wide.region_7.8_spmd.clone, body=%wide.region_4.7_spmd.clone.sunk | while | flops 17172484 | bytes 840889 | solution.py:218
  164.9 1.3 fusion.100
  171.6 1.3 fusion.100
  178.2 1.3 fusion.100
  184.9 1.3 fusion.100
  191.5 1.3 fusion.100
  198.2 1.3 fusion.100
  204.9 1.3 fusion.100
  208.0 2.5 fusion.76
  210.5 27.7 %while.29 = (s32[]{:T(128)}, f32[12,64,256]{2,1,0:T(8,128)}, s32[]{:T(128)}, bf16[8,12]{1,0:T(8,128)(2,1)}, bf16[8,12,64,256]{3,2,1,0:T(8,128)(2,1)}, /*index=5*/s32[]{:T(128)}, s32[]{:T(128)}) while((s32[]{:T(128)}, f32[12,64,256]{2,1,0:T(8,128)}, s32[]{:T(128)}, bf16[8,12]{1,0:T(8,128)(2,1)}, bf16[8,12,64,256]{3,2,1,0:T(8,128)(2,1)}, ...), condition=%wide.region_2.3_spmd.clone, body=%wide.region_1.2_spmd.clone.sunk | while | flops 983056 | bytes 1966305 | solution.py:40
  211.7 2.1 fusion.92
  215.0 2.3 fusion.92
  218.4 2.3 fusion.92
  221.9 2.3 fusion.92
  225.4 2.3 fusion.92
  228.9 2.3 fusion.92
  232.4 2.3 fusion.92
  235.8 2.3 fusion.92
  238.2 1.7 convolution_multiply_fusion.1
  239.9 2.7 %multiply_reduce_fusion = (f32[128,12]{0,1:T(8,128)S(1)}, f32[128,12,64]{0,2,1:T(8,128)S(1)}) fusion(f32[128,12,64]{0,2,1:T(8,128)} %bitcast.91, f32[128,12,64]{0,2,1:T(8,128)S(1)} %convolution_multiply_fusion.1, f32[12,128]{1,0:T(8,128)S(1)} %reduce_window_sum.11, f32[128,128]{1,0:T(8,128)S(1)} %fusion.66, pred[128,128]{1,0:T(8,128)(4,1)} %fusion.64, ...), kind=kOutput, calls=%fused_computation.69 | convolution fusion | flops 152173056 | bytes 1476608 | tf_op jit(solution)/shard_map/htj,jhd->thd/dot_general | solution.py:66
  243.5 1.4 fusion.20
  244.9 19.0 %reduce-scatter.2.cloned.1.call-done = bf16[128,512]{1,0:T(8,128)(2,1)} async-done(((bf16[128,2048]{1,0:T(8,128)(2,1)}), bf16[128,512]{1,0:T(8,128)(2,1)}) %reduce-scatter.2.cloned.1.call-update) | async-done | bytes 131088 | tf_op jit(solution)/shard_map/reduce_scatter | solution.py:229
  (164 shorter events, 74.5 us)
Async XLA Ops:
  6.5 237.0 %copy-start = (bf16[768,2048]{1,0:T(8,128)(2,1)S(1)}, bf16[768,2048]{1,0:T(8,128)(2,1)}, u32[]{:S(2)}) copy-start(bf16[768,2048]{1,0:T(8,128)(2,1)} %param.32) | copy-start | bytes 9437188
  6.5 89.1 %copy-start.6 = (bf16[128,256]{1,0:T(8,128)(2,1)S(1)}, bf16[128,256]{1,0:T(8,128)(2,1)}, u32[]{:S(2)}) copy-start(bf16[128,256]{1,0:T(8,128)(2,1)} %param.28) | copy-start | bytes 196612
  6.5 204.0 %all-gather.5.cloned.1.call-start = ((), (), s32[]{:S(2)}) async-start(), calls=%async_computation.2 | async-start | bytes 3538944 | tf_op jit(solution)/shard_map/all_gather | solution.py:23
  8.8 122.7 %collective-permute-start.3 = (bf16[128,128]{1,0:T(8,128)(2,1)}, bf16[128,128]{1,0:T(8,128)(2,1)}, u32[]{:S(2)}, u32[]{:S(2)}) collective-permute-start(bf16[128,128]{1,0:T(8,128)(2,1)} %get-tuple-element.278), channel_id=1, source_target_pairs={{0,4},{4,8},{8,12},{12,16},{16,20},{20,24},{24,28},{28,0},{1,5},{5... | collective-permute-start | bytes 98312 | tf_op jit(solution)/shard_map/ppermute | solution.py:170
  11.8 121.6 %collective-permute-start.4 = (bf16[128,128]{1,0:T(8,128)(2,1)}, bf16[128,128]{1,0:T(8,128)(2,1)}, u32[]{:S(2)}, u32[]{:S(2)}) collective-permute-start(bf16[128,128]{1,0:T(8,128)(2,1)} %get-tuple-element.278), channel_id=1, source_target_pairs={{0,28},{4,0},{8,4},{12,8},{16,12},{20,16},{24,20},{28,24},{1,29},{... | collective-permute-start | bytes 98312 | tf_op jit(solution)/shard_map/ppermute | solution.py:175
  16.7 81.2 %collective-permute-start.1 = (bf16[3]{0:T(256)(128)(2,1)}, bf16[3]{0:T(256)(128)(2,1)}, u32[]{:S(2)}, u32[]{:S(2)}) collective-permute-start(bf16[3]{0:T(256)(128)(2,1)} %slice.85), channel_id=1, source_target_pairs={{0,4},{4,8},{8,12},{12,16},{16,20},{20,24},{24,28},{1,5},{5,9},{9,... | collective-permute-start | bytes 26 | tf_op jit(solution)/shard_map/ppermute | solution.py:17
  19.8 103.2 %collective-permute-start.2 = (bf16[3,512]{1,0:T(4,128)(2,1)}, bf16[3,512]{1,0:T(4,128)(2,1)}, u32[]{:S(2)}, u32[]{:S(2)}) collective-permute-start(bf16[3,512]{1,0:T(4,128)(2,1)} %slice.95), channel_id=1, source_target_pairs={{0,4},{4,8},{8,12},{12,16},{16,20},{20,24},{24,28},{1,5},{5,9},{9,... | collective-permute-start | bytes 9224 | tf_op jit(solution)/shard_map/ppermute | solution.py:17
  25.4 100.0 %collective-permute-start = (bf16[3,768]{0,1:T(8,128)(2,1)}, bf16[3,768]{0,1:T(8,128)(2,1)}, u32[]{:S(2)}, u32[]{:S(2)}) collective-permute-start(bf16[3,768]{0,1:T(8,128)(2,1)} %copy.27), channel_id=1, source_target_pairs={{0,4},{4,8},{8,12},{12,16},{16,20},{20,24},{24,28},{1,5},{5,9},{9,... | collective-permute-start | bytes 13832 | tf_op jit(solution)/shard_map/ppermute | solution.py:17
  125.2 3.7 %copy-start.2 = (bf16[128,512]{1,0:T(8,128)(2,1)}, bf16[128,512]{1,0:T(8,128)(2,1)S(1)}, u32[]{:S(2)}) copy-start(bf16[128,512]{1,0:T(8,128)(2,1)S(1)} %multiply_convert_fusion.2) | copy-start | bytes 393220
  128.8 0.7 copy-start.4
  131.5 132.5 %reduce-scatter.2.cloned.1.call-start = ((), (), s32[]{:S(2)}) async-start(), calls=%async_computation.1 | async-start | bytes 655360 | tf_op jit(solution)/shard_map/reduce_scatter | solution.py:229
  131.5 7.5 %collective-permute-start.5 = (bf16[128,128]{1,0:T(8,128)(2,1)}, bf16[128,128]{1,0:T(8,128)(2,1)S(1)}, u32[]{:S(2)}, u32[]{:S(2)}) collective-permute-start(bf16[128,128]{1,0:T(8,128)(2,1)} %collective-permute-done.3), channel_id=1, source_target_pairs={{0,4},{4,8},{8,12},{12,16},{16,20},{20,24},{24,28},{28,0},{1,5},{5... | collective-permute-start | bytes 98312 | tf_op jit(solution)/shard_map/ppermute | solution.py:170
  133.4 5.6 %collective-permute-start.6 = (bf16[128,128]{1,0:T(8,128)(2,1)}, bf16[128,128]{1,0:T(8,128)(2,1)S(1)}, u32[]{:S(2)}, u32[]{:S(2)}) collective-permute-start(bf16[128,128]{1,0:T(8,128)(2,1)} %collective-permute-done.4), channel_id=1, source_target_pairs={{0,28},{4,0},{8,4},{12,8},{16,12},{20,16},{24,20},{28,24},{1,29},{... | collective-permute-start | bytes 98312 | tf_op jit(solution)/shard_map/ppermute | solution.py:175
  139.1 7.1 %collective-permute-start.7 = (bf16[128,128]{1,0:T(8,128)(2,1)S(1)}, bf16[128,128]{1,0:T(8,128)(2,1)S(1)}, u32[]{:S(2)}, u32[]{:S(2)}) collective-permute-start(bf16[128,128]{1,0:T(8,128)(2,1)S(1)} %collective-permute-done.5), channel_id=1, source_target_pairs={{0,4},{4,8},{8,12},{12,16},{16,20},{20,24},{24,28},{28,0},{1,5},{5... | collective-permute-start | bytes 98312 | tf_op jit(solution)/shard_map/ppermute | solution.py:170
  139.1 7.7 %collective-permute-start.8 = (bf16[128,128]{1,0:T(8,128)(2,1)S(1)}, bf16[128,128]{1,0:T(8,128)(2,1)S(1)}, u32[]{:S(2)}, u32[]{:S(2)}) collective-permute-start(bf16[128,128]{1,0:T(8,128)(2,1)S(1)} %collective-permute-done.6), channel_id=1, source_target_pairs={{0,28},{4,0},{8,4},{12,8},{16,12},{20,16},{24,20},{28,24},{1,29},{... | collective-permute-start | bytes 98312 | tf_op jit(solution)/shard_map/ppermute | solution.py:175
  146.2 7.3 %collective-permute-start.9 = (bf16[128,128]{1,0:T(8,128)(2,1)S(1)}, bf16[128,128]{1,0:T(8,128)(2,1)S(1)}, u32[]{:S(2)}, u32[]{:S(2)}) collective-permute-start(bf16[128,128]{1,0:T(8,128)(2,1)S(1)} %collective-permute-done.7), channel_id=1, source_target_pairs={{0,4},{4,8},{8,12},{12,16},{16,20},{20,24},{24,28},{28,0},{1,5},{5... | collective-permute-start | bytes 98312 | tf_op jit(solution)/shard_map/ppermute | solution.py:170
  210.5 27.7 %copy-start.3 = (bf16[128,512]{1,0:T(8,128)(2,1)S(1)}, bf16[128,512]{1,0:T(8,128)(2,1)}, u32[]{:S(2)}) copy-start(bf16[128,512]{1,0:T(8,128)(2,1)} %copy-done.2) | copy-start | bytes 393220
  210.5 29.4 %copy-start.5 = (bf16[128,768]{0,1:T(8,128)(2,1)S(1)}, bf16[128,768]{0,1:T(8,128)(2,1)}, u32[]{:S(2)}) copy-start(bf16[128,768]{0,1:T(8,128)(2,1)} %copy-done.4) | copy-start | bytes 589828
  210.5 29.4 %copy-start.7 = (f32[128,12]{0,1:T(8,128)S(1)}, f32[128,12]{0,1:T(8,128)}, u32[]{:S(2)}) copy-start(f32[128,12]{0,1:T(8,128)} %get-tuple-element.283) | copy-start | bytes 18436
  238.2 5.4 %copy-start.1 = (f32[128,2048]{1,0:T(8,128)S(1)}, f32[128,2048]{1,0:T(8,128)}, u32[]{:S(2)}) copy-start(f32[128,2048]{1,0:T(8,128)} %fusion.76) | copy-start | bytes 3145732
Sparse Core Ops, SparseCore 0:
  131.6 59.4 all-gather.4
  245.1 18.8 reduce-scatter.1
